TPU v7x, 256 devices: a whole 4x4x8 slice. The times are simulated.
256 devices in a mesh: grp: 4 (over y), row: 16 (over z, core), col: 4 (over x).
Axes of the slice: x: 4, y: 4, z: 8, core: 2. Of those that a mesh axis runs over, the one named last changes fastest.
Arguments:
- ocean_field: bfloat16 [256, 128, 128, 128], P('grp', 'row', 'col'), parts along dimension 0, may hold values from -6 to 6
- spec_first: bfloat16 [2, 32, 64, 64], replicated, may hold values from -0.5 to 0.5
- spec_second: bfloat16 [2, 32, 64, 64], replicated, may hold values from -0.5 to 0.5
- spec_third: bfloat16 [2, 32, 64, 64], replicated, may hold values from -0.5 to 0.5
- ffn_in: bfloat16 [64, 256], replicated, may hold values from -0.75 to 0.75
- ffn_out: bfloat16 [256, 64], replicated, may hold values from -0.375 to 0.375
- bias_in: float32 [256], replicated, may hold values from -3 to 3
- bias_out: float32 [64], replicated, may hold values from -3 to 3
Outputs:
- next_field: bfloat16 [256, 128, 128, 128], P('grp', 'row', 'col'), parts along dimension 0
There are 4 independent parts, one for each index of `grp`. A program takes and returns all parts, laid end to end along the dimension named above; an argument that names none is the same for every part. Nothing has to cross between parts.
All inputs are finite; a program needn't handle non-finite values.
Results may differ from a plain program's by a relative error of at most 0.013.
Values may be sent and summed in bfloat16 or wider, within the bound.
A program may use at most 128 MiB of HBM per device.

v0:
```python
import math

import jax
import jax.numpy as jnp
from jax import lax
from jax.sharding import PartitionSpec as P


def forward_table(length, mode_count):
    grid_pos = jnp.arange(length, dtype=jnp.int32)[:, None]
    mode_location = jnp.arange(mode_count, dtype=jnp.int32)[None, :]
    phase = (grid_pos * mode_location % length).astype(jnp.float32) * (2.0 * math.pi / length)
    return jnp.stack([jnp.cos(phase), -jnp.sin(phase)], axis=1).astype(jnp.bfloat16)


def inverse_table(length, mode_count):
    mode_location = jnp.arange(mode_count, dtype=jnp.int32)[:, None]
    grid_pos = jnp.arange(length, dtype=jnp.int32)[None, :]
    phase = (grid_pos * mode_location % length).astype(jnp.float32) * (2.0 * math.pi / length)
    factor = jnp.where(mode_location == 0, 1.0, 2.0).astype(jnp.float32) / length
    return jnp.stack([factor * jnp.cos(phase), -factor * jnp.sin(phase)], axis=0).astype(
        jnp.bfloat16
    )


def block_weight_tensor(weight_tensor):
    real_part = weight_tensor[0]
    imag_part = weight_tensor[1]
    upper = jnp.concatenate([real_part, imag_part], axis=2)
    lower = jnp.concatenate([-imag_part, real_part], axis=2)
    return jnp.concatenate([upper, lower], axis=1)


def along_axis(values, weight_tensor):
    channels, across, length, columns = values.shape
    mode_count = weight_tensor.shape[1]
    spectral_coefficients = jnp.einsum(
        "canq,nsm->mscaq",
        values,
        forward_table(length, mode_count),
        preferred_element_type=jnp.float32,
    )
    spectral_coefficients = spectral_coefficients.reshape(
        mode_count, 2 * channels, across * columns
    ).astype(jnp.bfloat16)
    mixed_result = jnp.einsum(
        "plf,plk->pkf",
        spectral_coefficients,
        block_weight_tensor(weight_tensor),
        preferred_element_type=jnp.float32,
    )
    mixed_result = mixed_result.astype(jnp.bfloat16).reshape(
        mode_count, 2, channels, across, columns
    )
    result = jnp.einsum(
        "mscaq,smn->canq",
        mixed_result,
        inverse_table(length, mode_count),
        preferred_element_type=jnp.float32,
    )
    return result.astype(jnp.bfloat16)


def final_axis_transform(values, weight_tensor):
    channels, places, length = values.shape
    mode_count = weight_tensor.shape[1]
    spectral_coefficients = jnp.einsum(
        "cpn,nsm->mscp",
        values,
        forward_table(length, mode_count),
        preferred_element_type=jnp.float32,
    )
    spectral_coefficients = spectral_coefficients.reshape(mode_count, 2 * channels, places).astype(
        jnp.bfloat16
    )
    mixed_result = jnp.einsum(
        "plf,plk->pkf",
        spectral_coefficients,
        block_weight_tensor(weight_tensor),
        preferred_element_type=jnp.float32,
    )
    mixed_result = mixed_result.astype(jnp.bfloat16).reshape(mode_count, 2, channels, places)
    result = jnp.einsum(
        "mscp,smn->cpn",
        mixed_result,
        inverse_table(length, mode_count),
        preferred_element_type=jnp.float32,
    )
    return result.astype(jnp.bfloat16)


def feed_forward(summed, initial, ffn_in, ffn_out, bias_in, bias_out):

    def update(position, output):
        row_index = jnp.asarray(position).astype(jnp.int32)
        block = lax.dynamic_index_in_dim(summed, row_index, 1, keepdims=False)
        base = lax.dynamic_index_in_dim(initial, row_index, 1, keepdims=False)
        hidden_pre = (
            jnp.einsum("ch,ck->hk", ffn_in, block, preferred_element_type=jnp.float32)
            + bias_in[:, None]
        )
        hidden = jax.nn.gelu(hidden_pre, approximate=False).astype(jnp.bfloat16)
        result = jnp.einsum("hc,hk->ck", ffn_out, hidden, preferred_element_type=jnp.float32)
        result = result + bias_out[:, None] + base.astype(jnp.float32)
        return lax.dynamic_update_index_in_dim(output, result.astype(jnp.bfloat16), row_index, 1)

    return lax.fori_loop(0, summed.shape[1], update, jnp.zeros_like(initial))


def body(ocean_field, spec_first, spec_second, spec_third, ffn_in, ffn_out, bias_in, bias_out):
    channels, row_cells, col_cells, line_cells = ocean_field.shape
    third_part = final_axis_transform(
        ocean_field.reshape(channels, row_cells * col_cells, line_cells), spec_third
    )
    third_part = third_part.reshape(ocean_field.shape)
    piece = lax.all_to_all(ocean_field, "row", split_axis=2, concat_axis=1, tiled=True)
    depth_a, full_rows, across, items = piece.shape
    lines = along_axis(piece.reshape(depth_a, 1, full_rows, across * items), spec_first)
    lines = lines.reshape(piece.shape)
    first_part = lax.all_to_all(lines, "row", split_axis=1, concat_axis=2, tiled=True)
    lines = along_axis(
        lax.all_to_all(ocean_field, "col", split_axis=1, concat_axis=2, tiled=True), spec_second
    )
    second_part = lax.all_to_all(lines, "col", split_axis=2, concat_axis=1, tiled=True)
    pair = (first_part.astype(jnp.float32) + second_part.astype(jnp.float32)).astype(jnp.bfloat16)
    summed = (pair.astype(jnp.float32) + third_part.astype(jnp.float32)).astype(jnp.bfloat16)
    flat_sum = summed.reshape(channels, row_cells, col_cells * line_cells)
    flat_field = ocean_field.reshape(channels, row_cells, col_cells * line_cells)
    result = feed_forward(flat_sum, flat_field, ffn_in, ffn_out, bias_in, bias_out)
    return result.reshape(ocean_field.shape)


def solution(mesh):
    return jax.shard_map(
        body,
        mesh=mesh,
        in_specs=(P("grp", "row", "col", None), P(), P(), P(), P(), P(), P(), P()),
        out_specs=P("grp", "row", "col", None),
        check_vma=False,
    )
```

profile of v0, /device:TPU:1, one launch (start us, length us, event | category | flops | bytes accessed | tf_op | source)
XLA Modules:
  0.0 462.4 jit_solution(5760468740737495977)
XLA Ops:
  0.0 5.0 %copy.55 = bf16[64,8,32,128]{3,2,0,1:T(8,128)(2,1)} copy(bf16[64,8,32,128]{3,2,1,0:T(8,128)(2,1)} %param.10) | data formatting | bytes 8388608 | tf_op args[0]
  9.9 5.8 %copy.47 = bf16[64,8,32,128]{3,1,0,2:T(8,128)(2,1)} copy(bf16[64,8,32,128]{3,2,1,0:T(8,128)(2,1)} %param.10) | data formatting | bytes 8388608 | tf_op args[0]
  15.7 41.0 %all-to-all-done.2 = bf16[64,8,32,128]{3,2,0,1:T(8,128)(2,1)} async-done(((bf16[64,8,32,128]{3,2,0,1:T(8,128)(2,1)}), bf16[64,8,32,128]{3,2,0,1:T(8,128)(2,1)}, u32[]{:S(2)}, u32[]{:S(2)}) %all-to-all-start.2) | async-done | bytes 4194336 | tf_op jit(solution)/shard_map/all_to_all | solution.py:122
  56.7 12.6 %all-to-all-start = ((bf16[64,8,32,128]{3,1,0,2:T(8,128)(2,1)}), bf16[64,8,32,128]{3,1,0,2:T(8,128)(2,1)}, u32[]{:S(2)}, u32[]{:S(2)}) async-start(bf16[64,8,32,128]{3,1,0,2:T(8,128)(2,1)} %copy.47), calls=%async_computation | async-start | bytes 8388608 | tf_op jit(solution)/shard_map/all_to_all | solution.py:116
  88.7 6.3 %copy.59 = bf16[64,2,128,128]{3,1,0,2:T(2,128)(2,1)} copy(bf16[64,2,128,128]{3,2,1,0:T(8,128)(2,1)S(1)} %fusion.92) | data formatting | bytes 8388608 | tf_op jit(solution)/shard_map/convert_element_type | solution.py:61
  95.0 67.7 %all-to-all-done = bf16[64,8,32,128]{3,1,0,2:T(8,128)(2,1)} async-done(((bf16[64,8,32,128]{3,1,0,2:T(8,128)(2,1)}), bf16[64,8,32,128]{3,1,0,2:T(8,128)(2,1)}, u32[]{:S(2)}, u32[]{:S(2)}) %all-to-all-start) | async-done | bytes 4194336 | tf_op jit(solution)/shard_map/all_to_all | solution.py:116
  162.8 5.3 %all-to-all-start.3 = ((bf16[64,2,128,128]{3,1,0,2:T(2,128)(2,1)}), bf16[64,2,128,128]{3,1,0,2:T(2,128)(2,1)}, u32[]{:S(2)}, u32[]{:S(2)}) async-start(bf16[64,2,128,128]{3,1,0,2:T(2,128)(2,1)} %copy.59), calls=%async_computation.3 | async-start | bytes 8388608 | tf_op jit(solution)/shard_map/all_to_all | solution.py:124
  177.1 6.9 %reshape.253 = bf16[64,128,2,128]{3,2,1,0:T(2,128)(2,1)} reshape(bf16[64,1,128,256]{3,2,0,1:T(8,128)(2,1)} %fusion.91) | data formatting | bytes 8388608 | tf_op jit(solution)/shard_map/reshape | solution.py:119
  184.0 8.9 %copy.51 = bf16[64,128,2,128]{3,2,0,1:T(2,128)(2,1)} copy(bf16[64,128,2,128]{3,2,1,0:T(2,128)(2,1)} %reshape.253) | data formatting | bytes 8388608 | tf_op jit(solution)/shard_map/reshape | solution.py:119
  192.9 23.2 %all-to-all-done.3 = bf16[64,2,128,128]{3,1,0,2:T(2,128)(2,1)} async-done(((bf16[64,2,128,128]{3,1,0,2:T(2,128)(2,1)}), bf16[64,2,128,128]{3,1,0,2:T(2,128)(2,1)}, u32[]{:S(2)}, u32[]{:S(2)}) %all-to-all-start.3) | async-done | bytes 4194336 | tf_op jit(solution)/shard_map/all_to_all | solution.py:124
  216.1 6.8 %all-to-all-start.1 = ((bf16[64,128,2,128]{3,2,0,1:T(2,128)(2,1)}), bf16[64,128,2,128]{3,2,0,1:T(2,128)(2,1)}, u32[]{:S(2)}, u32[]{:S(2)}) async-start(bf16[64,128,2,128]{3,2,0,1:T(2,128)(2,1)} %copy.51), calls=%async_computation.1 | async-start | bytes 8388608 | tf_op jit(solution)/shard_map/all_to_all | solution.py:120
  222.8 7.4 %reshape.275 = bf16[64,8,4096]{2,1,0:T(8,128)(2,1)} reshape(bf16[64,8,32,128]{3,2,1,0:T(8,128)(2,1)} %param.10) | data formatting | bytes 8388608 | tf_op jit(solution)/shard_map/reshape | solution.py:128
  236.4 5.0 %fusion.93 = f32[64,256,128]{2,1,0:T(8,128)} fusion(bf16[32,2,64,256]{3,2,1,0:T(8,128)(2,1)S(1)} %bitcast.221, bf16[1,32,128]{2,1,0:T(8,128)(2,1)S(1)} %get-tuple-element.169, bf16[1,32,128]{2,1,0:T(8,128)(2,1)S(1)} %get-tuple-element.170), kind=kOutput, calls=%fused_computation.104 | convolution fusion | flops 272637952 | bytes 10502144 | tf_op jit(solution)/shard_map/mscp,smn->cpn/dot_general | solution.py:83
  241.5 9.6 %reshape.262 = f32[64,8,4096]{2,1,0:T(8,128)} reshape(f32[64,256,128]{2,1,0:T(8,128)} %fusion.93) | data formatting | bytes 16777216 | tf_op jit(solution)/shard_map/convert_element_type | solution.py:126
  251.0 6.6 %copy.74 = bf16[64,8,4096]{2,0,1:T(8,128)(2,1)} copy(bf16[64,8,4096]{2,1,0:T(8,128)(2,1)} %reshape.275) | data formatting | bytes 8388608 | tf_op jit(solution)/shard_map/reshape | solution.py:128
  257.6 9.4 %convert_bitcast_fusion = f32[64,4,2,32,128]{4,2,0,3,1:T(2,128)} fusion(bf16[64,2,4,32,128]{4,1,0,3,2:T(2,128)(2,1)} %bitcast.62), kind=kLoop, calls=%fused_computation.94 | loop fusion | flops 2097152 | bytes 12582912 | tf_op jit(solution)/shard_map/convert_element_type | solution.py:125
  266.9 11.5 %copy.60 = f32[64,4,2,32,128]{4,3,0,2,1:T(8,128)} copy(f32[64,4,2,32,128]{4,2,0,3,1:T(2,128)} %convert_bitcast_fusion) | data formatting | bytes 16777216 | tf_op jit(solution)/shard_map/convert_element_type | solution.py:125
  278.4 9.5 %reshape.261 = f32[64,8,4096]{2,0,1:T(8,128)} reshape(f32[64,4,2,32,128]{4,3,0,2,1:T(8,128)} %copy.60) | data formatting | bytes 16777216 | tf_op jit(solution)/shard_map/convert_element_type | solution.py:125
  288.0 28.4 %all-to-all-done.1 = bf16[64,128,2,128]{3,2,0,1:T(2,128)(2,1)} async-done(((bf16[64,128,2,128]{3,2,0,1:T(2,128)(2,1)}), bf16[64,128,2,128]{3,2,0,1:T(2,128)(2,1)}, u32[]{:S(2)}, u32[]{:S(2)}) %all-to-all-start.1) | async-done | bytes 4194336 | tf_op jit(solution)/shard_map/all_to_all | solution.py:120
  316.4 9.4 %convert_bitcast_fusion.1 = f32[64,8,16,2,128]{4,3,0,1,2:T(2,128)} fusion(bf16[64,16,8,2,128]{4,3,0,2,1:T(2,128)(2,1)} %bitcast.57), kind=kLoop, calls=%fused_computation.95 | loop fusion | flops 2097152 | bytes 12582912 | tf_op jit(solution)/shard_map/convert_element_type | solution.py:125
  325.8 8.6 %copy.52 = f32[64,8,16,2,128]{4,3,2,0,1:T(2,128)} copy(f32[64,8,16,2,128]{4,3,0,1,2:T(2,128)} %convert_bitcast_fusion.1) | data formatting | bytes 16777216 | tf_op jit(solution)/shard_map/convert_element_type | solution.py:125
  334.4 11.5 %reshape.260 = f32[64,8,4096]{2,0,1:T(8,128)} reshape(f32[64,8,16,2,128]{4,3,2,0,1:T(2,128)} %copy.52) | data formatting | bytes 16777216 | tf_op jit(solution)/shard_map/convert_element_type | solution.py:125
  345.9 12.9 %fusion.90 = bf16[64,8,4096]{2,0,1:T(8,128)(2,1)} fusion(f32[64,8,4096]{2,1,0:T(8,128)} %reshape.262, f32[64,8,4096]{2,0,1:T(8,128)} %reshape.260, f32[64,8,4096]{2,0,1:T(8,128)} %reshape.261), kind=kLoop, calls=%fused_computation.100 | loop fusion | flops 10485760 | bytes 29360128 | tf_op jit(solution)/shard_map/convert_element_type | solution.py:126
  358.9 96.5 %while.13 = (s32[]{:T(128)}, bf16[64,8,4096]{2,0,1:T(8,128)(2,1)}, bf16[64,8,4096]{2,0,1:T(8,128)(2,1)}, bf16[64,256]{1,0:T(8,128)(2,1)S(1)}, f32[256]{0:T(256)S...) while((s32[]{:T(128)}, bf16[64,8,4096]{2,0,1:T(8,128)(2,1)}, ...), condition=%wide.region_1.2_spmd, body=%wide.region_0.1_spmd.sunk | while | flops 338690048 | bytes 1640797 | solution.py:107
  359.1 12.0 %fusion.180 = bf16[64,8,4096]{2,0,1:T(8,128)(2,1)} fusion(bf16[64,8,4096]{2,0,1:T(8,128)(2,1)} %get-tuple-element.230, s32[]{:T(128)} %get-tuple-element.229, bf16[256,64]{0,1:T(8,128)(2,1)S(1)} %get-tuple-element.243, bf16[64,256]{1,0:T(8,128)(2,1)S(1)} %get-tuple-element.241, f32[256]{0:T(256)S(1)} %get-tuple-element.242, ...), kind=kOutput, calls=%fused_computation.7.clone.1 | convolution fusion | flops 338690048 | bytes 1640704 | tf_op jit(solution)/shard_map/while/body/eval_jaxpr/hc,hk->ck/dot_general | solution.py:103
  371.2 12.0 %fusion.180 = bf16[64,8,4096]{2,0,1:T(8,128)(2,1)} fusion(bf16[64,8,4096]{2,0,1:T(8,128)(2,1)} %get-tuple-element.230, s32[]{:T(128)} %get-tuple-element.229, bf16[256,64]{0,1:T(8,128)(2,1)S(1)} %get-tuple-element.243, bf16[64,256]{1,0:T(8,128)(2,1)S(1)} %get-tuple-element.241, f32[256]{0:T(256)S(1)} %get-tuple-element.242, ...), kind=kOutput, calls=%fused_computation.7.clone.1 | convolution fusion | flops 338690048 | bytes 1640704 | tf_op jit(solution)/shard_map/while/body/eval_jaxpr/hc,hk->ck/dot_general | solution.py:103
  383.2 12.0 %fusion.180 = bf16[64,8,4096]{2,0,1:T(8,128)(2,1)} fusion(bf16[64,8,4096]{2,0,1:T(8,128)(2,1)} %get-tuple-element.230, s32[]{:T(128)} %get-tuple-element.229, bf16[256,64]{0,1:T(8,128)(2,1)S(1)} %get-tuple-element.243, bf16[64,256]{1,0:T(8,128)(2,1)S(1)} %get-tuple-element.241, f32[256]{0:T(256)S(1)} %get-tuple-element.242, ...), kind=kOutput, calls=%fused_computation.7.clone.1 | convolution fusion | flops 338690048 | bytes 1640704 | tf_op jit(solution)/shard_map/while/body/eval_jaxpr/hc,hk->ck/dot_general | solution.py:103
  395.3 12.0 %fusion.180 = bf16[64,8,4096]{2,0,1:T(8,128)(2,1)} fusion(bf16[64,8,4096]{2,0,1:T(8,128)(2,1)} %get-tuple-element.230, s32[]{:T(128)} %get-tuple-element.229, bf16[256,64]{0,1:T(8,128)(2,1)S(1)} %get-tuple-element.243, bf16[64,256]{1,0:T(8,128)(2,1)S(1)} %get-tuple-element.241, f32[256]{0:T(256)S(1)} %get-tuple-element.242, ...), kind=kOutput, calls=%fused_computation.7.clone.1 | convolution fusion | flops 338690048 | bytes 1640704 | tf_op jit(solution)/shard_map/while/body/eval_jaxpr/hc,hk->ck/dot_general | solution.py:103
  407.3 12.0 %fusion.180 = bf16[64,8,4096]{2,0,1:T(8,128)(2,1)} fusion(bf16[64,8,4096]{2,0,1:T(8,128)(2,1)} %get-tuple-element.230, s32[]{:T(128)} %get-tuple-element.229, bf16[256,64]{0,1:T(8,128)(2,1)S(1)} %get-tuple-element.243, bf16[64,256]{1,0:T(8,128)(2,1)S(1)} %get-tuple-element.241, f32[256]{0:T(256)S(1)} %get-tuple-element.242, ...), kind=kOutput, calls=%fused_computation.7.clone.1 | convolution fusion | flops 338690048 | bytes 1640704 | tf_op jit(solution)/shard_map/while/body/eval_jaxpr/hc,hk->ck/dot_general | solution.py:103
  419.3 12.0 %fusion.180 = bf16[64,8,4096]{2,0,1:T(8,128)(2,1)} fusion(bf16[64,8,4096]{2,0,1:T(8,128)(2,1)} %get-tuple-element.230, s32[]{:T(128)} %get-tuple-element.229, bf16[256,64]{0,1:T(8,128)(2,1)S(1)} %get-tuple-element.243, bf16[64,256]{1,0:T(8,128)(2,1)S(1)} %get-tuple-element.241, f32[256]{0:T(256)S(1)} %get-tuple-element.242, ...), kind=kOutput, calls=%fused_computation.7.clone.1 | convolution fusion | flops 338690048 | bytes 1640704 | tf_op jit(solution)/shard_map/while/body/eval_jaxpr/hc,hk->ck/dot_general | solution.py:103
  431.4 12.0 %fusion.180 = bf16[64,8,4096]{2,0,1:T(8,128)(2,1)} fusion(bf16[64,8,4096]{2,0,1:T(8,128)(2,1)} %get-tuple-element.230, s32[]{:T(128)} %get-tuple-element.229, bf16[256,64]{0,1:T(8,128)(2,1)S(1)} %get-tuple-element.243, bf16[64,256]{1,0:T(8,128)(2,1)S(1)} %get-tuple-element.241, f32[256]{0:T(256)S(1)} %get-tuple-element.242, ...), kind=kOutput, calls=%fused_computation.7.clone.1 | convolution fusion | flops 338690048 | bytes 1640704 | tf_op jit(solution)/shard_map/while/body/eval_jaxpr/hc,hk->ck/dot_general | solution.py:103
  443.4 12.0 %fusion.180 = bf16[64,8,4096]{2,0,1:T(8,128)(2,1)} fusion(bf16[64,8,4096]{2,0,1:T(8,128)(2,1)} %get-tuple-element.230, s32[]{:T(128)} %get-tuple-element.229, bf16[256,64]{0,1:T(8,128)(2,1)S(1)} %get-tuple-element.243, bf16[64,256]{1,0:T(8,128)(2,1)S(1)} %get-tuple-element.241, f32[256]{0:T(256)S(1)} %get-tuple-element.242, ...), kind=kOutput, calls=%fused_computation.7.clone.1 | convolution fusion | flops 338690048 | bytes 1640704 | tf_op jit(solution)/shard_map/while/body/eval_jaxpr/hc,hk->ck/dot_general | solution.py:103
  (46 shorter events, 46.1 us)
Async XLA Ops:
  5.0 51.7 %all-to-all-start.2 = ((bf16[64,8,32,128]{3,2,0,1:T(8,128)(2,1)}), bf16[64,8,32,128]{3,2,0,1:T(8,128)(2,1)}, u32[]{:S(2)}, u32[]{:S(2)}) async-start(bf16[64,8,32,128]{3,2,0,1:T(8,128)(2,1)} %copy.55), calls=%async_computation.2 | async-start | bytes 8388608 | tf_op jit(solution)/shard_map/all_to_all | solution.py:122
  15.7 53.6 %copy-start = (bf16[2,32,64,64]{3,2,1,0:T(8,128)(2,1)S(1)}, bf16[2,32,64,64]{3,2,1,0:T(8,128)(2,1)}, u32[]{:S(2)}) copy-start(bf16[2,32,64,64]{3,2,1,0:T(8,128)(2,1)} %param.12) | copy-start | bytes 1572868
  56.7 106.0 %all-to-all-start = ((bf16[64,8,32,128]{3,1,0,2:T(8,128)(2,1)}), bf16[64,8,32,128]{3,1,0,2:T(8,128)(2,1)}, u32[]{:S(2)}, u32[]{:S(2)}) async-start(bf16[64,8,32,128]{3,1,0,2:T(8,128)(2,1)} %copy.47), calls=%async_computation | async-start | bytes 8388608 | tf_op jit(solution)/shard_map/all_to_all | solution.py:116
  95.0 73.0 %copy-start.1 = (bf16[2,32,64,64]{3,2,1,0:T(8,128)(2,1)S(1)}, bf16[2,32,64,64]{3,2,1,0:T(8,128)(2,1)}, u32[]{:S(2)}) copy-start(bf16[2,32,64,64]{3,2,1,0:T(8,128)(2,1)} %param.11) | copy-start | bytes 1572868
  162.8 53.3 %all-to-all-start.3 = ((bf16[64,2,128,128]{3,1,0,2:T(2,128)(2,1)}), bf16[64,2,128,128]{3,1,0,2:T(2,128)(2,1)}, u32[]{:S(2)}, u32[]{:S(2)}) async-start(bf16[64,2,128,128]{3,1,0,2:T(2,128)(2,1)} %copy.59), calls=%async_computation.3 | async-start | bytes 8388608 | tf_op jit(solution)/shard_map/all_to_all | solution.py:124
  216.1 100.4 %all-to-all-start.1 = ((bf16[64,128,2,128]{3,2,0,1:T(2,128)(2,1)}), bf16[64,128,2,128]{3,2,0,1:T(2,128)(2,1)}, u32[]{:S(2)}, u32[]{:S(2)}) async-start(bf16[64,128,2,128]{3,2,0,1:T(2,128)(2,1)} %copy.51), calls=%async_computation.1 | async-start | bytes 8388608 | tf_op jit(solution)/shard_map/all_to_all | solution.py:120
  222.8 7.4 %copy-start.2 = (bf16[2,32,64,64]{3,2,1,0:T(8,128)(2,1)S(1)}, bf16[2,32,64,64]{3,2,1,0:T(8,128)(2,1)}, u32[]{:S(2)}) copy-start(bf16[2,32,64,64]{3,2,1,0:T(8,128)(2,1)} %param.13) | copy-start | bytes 1572868
  345.9 13.0 %copy-start.3 = (bf16[64,256]{1,0:T(8,128)(2,1)S(1)}, bf16[64,256]{1,0:T(8,128)(2,1)}, u32[]{:S(2)}) copy-start(bf16[64,256]{1,0:T(8,128)(2,1)} %param.14) | copy-start | bytes 98308
  345.9 13.0 %copy-start.4 = (bf16[256,64]{0,1:T(8,128)(2,1)S(1)}, bf16[256,64]{0,1:T(8,128)(2,1)}, u32[]{:S(2)}) copy-start(bf16[256,64]{0,1:T(8,128)(2,1)} %param.15) | copy-start | bytes 98308
  345.9 13.0 %copy-start.5 = (f32[256]{0:T(256)S(1)}, f32[256]{0:T(256)}, u32[]{:S(2)}) copy-start(f32[256]{0:T(256)} %param.16) | copy-start | bytes 3076
  345.9 13.0 %copy-start.6 = (f32[64]{0:T(128)S(1)}, f32[64]{0:T(128)}, u32[]{:S(2)}) copy-start(f32[64]{0:T(128)} %param.17) | copy-start | bytes 772
where the time goes:
time: 467 us; the launch traced here: 462 us
  waiting for transfers between devices  160 us (34%)
  matrix products  122 us (26%)
  local copies, waits for them, and re-layouts  117 us (25%)
  other arithmetic  32.9 us (7%)
  starting transfers between devices  29.5 us (6%)
    dot_general x8, matrix products, update(): jnp.einsum('hc,hk->ck', ffn_out, hidden, preferred_element_type=jnp.float32)  96.3 us
    all_to_all x1, waiting for transfers between devices, body(): lax.all_to_all(ocean_field, 'row', split_axis=2, concat_axis=1, tiled=True)  67.7 us
    all_to_all x1, waiting for transfers between devices, body(): lax.all_to_all(ocean_field, 'col', split_axis=1, concat_axis=2, tiled=True)  41 us
    all_to_all x1, waiting for transfers between devices, body(): lax.all_to_all(lines, 'row', split_axis=1, concat_axis=2, tiled=True)  28.4 us
    all_to_all x1, waiting for transfers between devices, body(): lax.all_to_all(lines, 'col', split_axis=2, concat_axis=1, tiled=True)  23.2 us
    convert_element_type x2, local copies, waits for them, and re-layouts, body(): second_part.astype(jnp.float32)  21 us
    convert_element_type x2, local copies, waits for them, and re-layouts, body(): first_part.astype(jnp.float32) + second_part.astype(jnp.float32)  20.1 us
    unnamed x23, local copies, waits for them, and re-layouts  16 us
  transfers between devices with their start and end apart: 4, of which 4 were waited for; matrix products, arithmetic and copies ran while one was open for 26% of the time, Pallas kernels for 0%

commit v1 on v0

v1 whole, which is shorter than its diff:
```python
import functools
import math

import jax
import jax.numpy as jnp
import ml_dtypes
import numpy as np
from jax import lax
from jax.experimental import pallas as pl
from jax.experimental.pallas import tpu as pltpu
from jax.sharding import PartitionSpec as P

MESH = pl.DeviceIdType.MESH
BF = jnp.bfloat16
F32 = jnp.float32
ROOT_HALF = math.sqrt(0.5)
ORDER = (8, 7, 9, 6, 10, 5, 11, 4, 12, 3, 13, 2, 14, 1, 15)


def tables(length, modes):
    n = np.arange(length, dtype=np.int32)[:, None]
    m = np.arange(modes, dtype=np.int32)[None, :]
    phase = (n * m % length).astype(np.float32) * np.float32(2.0 * math.pi / length)
    cos, sin = np.cos(phase).astype(np.float32), np.sin(phase).astype(np.float32)
    forward = np.stack([cos, -sin], axis=2).reshape(length, 2 * modes)
    factor = (np.where(m == 0, 1.0, 2.0) / length).astype(np.float32)
    inverse = np.stack([factor * cos, -factor * sin], axis=2).reshape(length, 2 * modes)
    return forward.astype(ml_dtypes.bfloat16), inverse.astype(ml_dtypes.bfloat16)


def constants(length, modes, rows, peers, half):
    forward, inverse = (t.astype(np.float32) for t in tables(length, modes))
    eye = np.eye(8, dtype=np.float32)
    k = 2 * modes
    split = forward.reshape(peers, rows, k)
    fwd_row = np.einsum("pnk,cd->kcpdn", split, eye).reshape(k * 8, length * 8)
    fwd_col = np.einsum("nk,cd->kcdn", forward, eye).reshape(k * 8, length * 8)
    split = inverse.reshape(peers, rows, k)
    inv_row = np.einsum("pnk,cd->pcnkd", split, eye).reshape(length * 8, k * 8)
    inv_col = np.einsum("nk,cd->cnkd", inverse, eye).reshape(length * 8, k * 8)
    inv_line = np.ascontiguousarray(inv_col.T)
    swap = np.zeros((half, 2, rows, 2, rows, half), np.float32)
    place = np.zeros((half, rows, rows, half), np.float32)
    for a in range(half):
        for b in range(rows):
            place[a, b, b, a] = 1.0
            for c in range(2):
                swap[a, c, b, c, b, a] = 1.0
    swap = swap.reshape(2 * half * rows, 2 * half * rows)
    place = place.reshape(half * rows, half * rows)
    return [t.astype(ml_dtypes.bfloat16) for t in (fwd_row, inv_row, fwd_col, inv_col, inv_line, swap, place)]


def dot(a, b):
    return jnp.dot(a, b, preferred_element_type=F32)


def dot_nt(a, b):
    return lax.dot_general(a, b, (((1,), (1,)), ((), ())), preferred_element_type=F32)


def dot_tn(a, b):
    return lax.dot_general(a, b, (((0,), (0,)), ((), ())), preferred_element_type=F32)


def loop(count, body, wide=1):
    def step(i, carry):
        for j in range(wide):
            body(i * wide + j)
        return carry

    lax.fori_loop(0, count // wide, step, 0)


def kernel(
    x_hbm, s1_hbm, s2_hbm, s3_hbm, ffn_in, ffn_out, bias_in, bias_out,
    fr_hbm, ir_hbm, fc_hbm, ic_hbm, il_hbm, swap, place,
    out_hbm,
    x, xs, ra, rb, back1, back2, third, spec, mix_w, fr, ir, fc, ic, il,
    widen_in, widen_out, wide_in, wide_out, hidden,
    load_sem, own_sem, out_sem, fwd_s, fwd_r, ret_s, ret_r, cf_s, cf_r, cr_s, cr_r,
):
    g, r, q = lax.axis_index("grp"), lax.axis_index("row"), lax.axis_index("col")
    loads = [
        pltpu.make_async_copy(src, dst, load_sem.at[i])
        for i, (src, dst) in enumerate(
            [
                (x_hbm, x), (s3_hbm, mix_w.at[0]), (fc_hbm, fc), (il_hbm, il), (fr_hbm, fr),
                (ir_hbm, ir), (ic_hbm, ic), (s1_hbm, mix_w.at[1]), (s2_hbm, mix_w.at[2]),
            ]
        )
    ]
    for c in loads:
        c.start()

    barrier = pltpu.get_barrier_semaphore()
    for d in range(1, 16):
        pl.semaphore_signal(barrier, inc=1, device_id=(g, lax.rem(r + d, 16), q), device_id_type=MESH)
    for d in range(1, 4):
        pl.semaphore_signal(barrier, inc=1, device_id=(g, r, lax.rem(q + d, 4)), device_id_type=MESH)

    def forward(k, t, s):
        return pltpu.make_async_remote_copy(
            xs.at[k * 16 + t], ra.at[k, s], fwd_s.at[k, t], fwd_r.at[k, s], device_id=(g, t, q), device_id_type=MESH
        )

    def give(k, t, s):
        return pltpu.make_async_remote_copy(
            ra.at[k, t], back1.at[k * 16 + s], ret_s.at[k, t], ret_r.at[k, s], device_id=(g, t, q), device_id_type=MESH
        )

    def col_forward(k, t, s):
        return pltpu.make_async_remote_copy(
            x.at[:, 2 * t + k], rb.at[k, :, s], cf_s.at[k, t], cf_r.at[k, s], device_id=(g, r, t), device_id_type=MESH
        )

    def col_give(k, t, s):
        return pltpu.make_async_remote_copy(
            rb.at[k, :, t], back2.at[:, 2 * s + k], cr_s.at[k, t], cr_r.at[k, s], device_id=(g, r, t), device_id_type=MESH
        )

    own = [pltpu.make_async_copy(xs.at[k * 16 + r], ra.at[k, r], own_sem.at[k]) for k in range(2)]
    own_back = [pltpu.make_async_copy(ra.at[k, r], back1.at[k * 16 + r], own_sem.at[2 + k]) for k in range(2)]
    own_col = [pltpu.make_async_copy(x.at[:, 2 * q + k], rb.at[k, :, q], own_sem.at[4 + k]) for k in range(2)]
    own_col_back = [
        pltpu.make_async_copy(rb.at[k, :, q], back2.at[:, 2 * q + k], own_sem.at[6 + k]) for k in range(2)
    ]

    def swapped(ref, k, i):
        parts = [
            ref[pl.ds(4 * i + 2 * j, 2), :, pl.ds(16 * k, 16), :].reshape(256, 128) for j in range(2)
        ]
        both = dot(swap[...], jnp.concatenate(parts, axis=1))
        return [both[:, 128 * j : 128 * (j + 1)].reshape(16, 16, 128) for j in range(2)]

    def to_rows(k):
        def step(i):
            for j, part in enumerate(swapped(x, k, i)):
                xs[pl.ds(16 * k, 16), pl.ds(32 * i + 16 * j, 16), :] = part.astype(BF)

        loop(16, step, 2)

    loads[0].wait()
    to_rows(0)
    pl.semaphore_wait(barrier, 18)
    for d in ORDER:
        forward(0, lax.rem(r + d, 16), r).start()
    own[0].start()
    for k in range(2):
        own_col[k].start()
        for d in range(1, 4):
            col_forward(k, lax.rem(q + d, 4), q).start()
    to_rows(1)
    for d in ORDER:
        forward(1, lax.rem(r + d, 16), r).start()
    own[1].start()

    def transposed_mix(d):
        def step(m):
            re = mix_w[d, 0, m].astype(F32)
            im = mix_w[d, 1, m].astype(F32)
            upper = jnp.concatenate([re, im], axis=1)
            lower = jnp.concatenate([-im, re], axis=1)
            return jnp.concatenate([upper, lower], axis=0).T.astype(BF)

        return step

    def mix(d):
        matrix = transposed_mix(d)

        def step(m):
            rhs = spec[pl.ds(2 * m, 2)].reshape(128, 128).astype(BF)
            spec[pl.ds(2 * m, 2)] = dot(matrix(m), rhs).reshape(2, 64, 128)

        loop(32, step, 2)

    def fold(i, result):
        spec[:, pl.ds(8 * i, 8), :] = result.reshape(64, 8, 128)

    def unfold(i):
        return spec[:, pl.ds(8 * i, 8), :].reshape(512, 128).astype(BF)

    def branch_third(k):
        def ahead(i):
            lanes = [
                x[8 * i + j, :, pl.ds(16 * k, 16), :].reshape(128, 128) for j in range(8)
            ]
            fold(i, dot_nt(fc[...], jnp.concatenate(lanes, axis=1)))

        loop(8, ahead)
        mix(0)

        def behind(i):
            turned = dot_nt(place[...], unfold(i)).astype(BF)
            result = dot(turned, il[...])
            for j in range(4):
                pair = [
                    result[:, 128 * (2 * j + e) : 128 * (2 * j + e + 1)].reshape(16, 8, 128) for e in range(2)
                ]
                third[pl.ds(16 * k, 16), pl.ds(64 * i + 16 * j, 16), :] = jnp.concatenate(pair, axis=1).astype(BF)

        loop(8, behind)

    def branch_first(k):
        def ahead(i):
            fold(i, dot(fr[...], ra[k, :, pl.ds(64 * i, 64), :].reshape(1024, 128)))

        loop(8, ahead)
        mix(1)

        def behind(i):
            ra[k, :, pl.ds(64 * i, 64), :] = dot(ir[...], unfold(i)).astype(BF).reshape(16, 64, 128)

        loop(8, behind)

    def branch_second(k):
        def ahead(i):
            fold(i, dot(fc[...], rb[k, pl.ds(8 * i, 8)].reshape(1024, 128)))

        loop(8, ahead)
        mix(2)

        def behind(i):
            rb[k, pl.ds(8 * i, 8)] = dot(ic[...], unfold(i)).astype(BF).reshape(8, 4, 32, 128)

        loop(8, behind)

    for i in (1, 2, 3):
        loads[i].wait()
    branch_third(0)
    branch_third(1)

    def spread(rows, columns):
        a = lax.broadcasted_iota(jnp.int32, (rows, columns), 0)
        b = lax.broadcasted_iota(jnp.int32, (rows, columns), 1)
        return (b // 8 == a).astype(F32).astype(BF)

    def diagonal(columns):
        a = lax.broadcasted_iota(jnp.int32, (8, columns), 0)
        b = lax.broadcasted_iota(jnp.int32, (8, columns), 1)
        return (b % 8 == a).astype(F32)

    widen_in[...] = dot_tn(ffn_in[...], spread(64, 512))
    widen_out[...] = dot_tn(ffn_out[...], spread(256, 2048))

    def widen(src, dst, columns):
        keep = diagonal(columns)

        def step(i):
            pair = [jnp.broadcast_to(src[pl.ds(2 * i + e, 1), :], (8, columns)) * keep for e in range(2)]
            dst[pl.ds(16 * i, 16), :] = jnp.concatenate(pair, axis=0).astype(BF)

        return step

    loop(128, widen(widen_in, wide_in, 512))
    loop(32, widen(widen_out, wide_out, 2048))

    for i in range(4, 9):
        loads[i].wait()

    def do_first(k):
        own[k].wait()
        for d in ORDER:
            forward(k, r, lax.rem(r + 16 - d, 16)).wait_recv()
        branch_first(k)
        for d in ORDER:
            give(k, lax.rem(r + d, 16), r).start()
        own_back[k].start()

    def do_second(k):
        own_col[k].wait()
        for d in range(1, 4):
            col_forward(k, q, lax.rem(q + d, 4)).wait_recv()
        branch_second(k)
        for d in range(1, 4):
            col_give(k, lax.rem(q + d, 4), q).start()
        own_col_back[k].start()

    do_first(0)
    do_second(0)
    do_second(1)
    do_first(1)

    for k in range(2):
        own_col_back[k].wait()
        for d in range(1, 4):
            col_give(k, q, lax.rem(q + d, 4)).wait_recv()
        for d in range(1, 4):
            col_forward(k, lax.rem(q + d, 4), q).wait_send()
        for d in ORDER:
            forward(k, lax.rem(r + d, 16), r).wait_send()

    def add_second(k):
        def step(i):
            for j, part in enumerate(swapped(back2, k, i)):
                at = (pl.ds(16 * k, 16), pl.ds(32 * i + 16 * j, 16), slice(None))
                third[at] = (third[at].astype(F32) + part).astype(BF)

        loop(16, step, 2)

    add_second(0)
    add_second(1)

    def feed(first, second):
        both = (first, second)
        lanes = [(back1[n].astype(F32) + third[n].astype(F32)).astype(BF) for n in both]
        summed = jnp.concatenate(lanes, axis=1)

        def up(i):
            at = pl.ds(256 * i, 256)
            pre = dot(wide_in[at, :], summed)
            bias = bias_in[at, :]
            pre = pre + jnp.concatenate([bias, bias], axis=1)
            hidden[at, :] = (0.5 * pre * (1.0 + lax.erf(pre * ROOT_HALF))).astype(BF)

        loop(8, up)

        def down(i):
            at = pl.ds(128 * i, 128)
            result = dot(wide_out[at, :], hidden[...])
            for j, n in enumerate(both):
                part = result[:, 128 * j : 128 * (j + 1)] + bias_out[at, :] + xs[n, at, :].astype(F32)
                xs[n, at, :] = part.astype(BF)

        loop(4, down)
        for n in both:
            pltpu.make_async_copy(xs.at[n], out_hbm.at[n], out_sem.at[n]).start()

    for k in range(2):
        own_back[k].wait()
        steps = (0,) + ORDER
        for i in range(8):
            sources = [lax.rem(r + 16 - d, 16) for d in steps[2 * i : 2 * i + 2]]
            for d, s in zip(steps[2 * i : 2 * i + 2], sources):
                if d:
                    give(k, r, s).wait_recv()
            feed(16 * k + sources[0], 16 * k + sources[1])

    for n in range(32):
        pltpu.make_async_copy(xs.at[n], out_hbm.at[n], out_sem.at[n]).wait()
    for k in range(2):
        for d in range(1, 4):
            col_give(k, lax.rem(q + d, 4), q).wait_send()
        for d in ORDER:
            give(k, lax.rem(r + d, 16), r).wait_send()


def body(ocean_field, spec_first, spec_second, spec_third, ffn_in, ffn_out, bias_in, bias_out):
    consts = constants(128, 32, 8, 16, 16)
    wide_bias_in = jnp.broadcast_to(jnp.repeat(bias_in, 8)[:, None], (2048, 128))
    wide_bias_out = jnp.broadcast_to(jnp.repeat(bias_out, 8)[:, None], (512, 128))
    anywhere, vmem = pl.BlockSpec(memory_space=pl.ANY), pl.BlockSpec(memory_space=pltpu.VMEM)
    dma = pltpu.SemaphoreType.DMA
    scratch = [
        pltpu.VMEM((64, 8, 32, 128), BF),
        pltpu.VMEM((32, 512, 128), BF),
        pltpu.VMEM((2, 16, 512, 128), BF),
        pltpu.VMEM((2, 64, 4, 32, 128), BF),
        pltpu.VMEM((32, 512, 128), BF),
        pltpu.VMEM((64, 8, 32, 128), BF),
        pltpu.VMEM((32, 512, 128), BF),
        pltpu.VMEM((64, 64, 128), F32),
        pltpu.VMEM((3, 2, 32, 64, 64), BF),
        pltpu.VMEM((512, 1024), BF),
        pltpu.VMEM((1024, 512), BF),
        pltpu.VMEM((512, 1024), BF),
        pltpu.VMEM((1024, 512), BF),
        pltpu.VMEM((512, 1024), BF),
        pltpu.VMEM((256, 512), F32),
        pltpu.VMEM((64, 2048), F32),
        pltpu.VMEM((2048, 512), BF),
        pltpu.VMEM((512, 2048), BF),
        pltpu.VMEM((2048, 256), BF),
        dma((9,)), dma((8,)), dma((32,)),
        dma((2, 16)), dma((2, 16)), dma((2, 16)), dma((2, 16)),
        dma((2, 4)), dma((2, 4)), dma((2, 4)), dma((2, 4)),
    ]
    result = pl.pallas_call(
        kernel,
        out_shape=jax.ShapeDtypeStruct((32, 512, 128), BF),
        in_specs=[anywhere] * 4 + [vmem] * 4 + [anywhere] * 5 + [vmem] * 2,
        out_specs=anywhere,
        scratch_shapes=scratch,
        compiler_params=pltpu.CompilerParams(
            collective_id=0, has_side_effects=True, vmem_limit_bytes=60 * 2**20
        ),
        name="fno_layer",
    )(
        ocean_field, spec_first, spec_second, spec_third, ffn_in, ffn_out, wide_bias_in, wide_bias_out,
        *[jnp.asarray(c) for c in consts],
    )
    return result.reshape(32, 64, 8, 128).transpose(1, 2, 0, 3)


def solution(mesh):
    return jax.shard_map(
        body,
        mesh=mesh,
        in_specs=(P("grp", "row", "col", None), P(), P(), P(), P(), P(), P(), P()),
        out_specs=P("grp", "row", "col", None),
        check_vma=False,
    )
```

time: 467 us -> 218 us (0.47)
  Pallas kernels: 0 us -> 203 us
  waiting for transfers between devices: 160 us -> 0 us
  matrix products: 122 us -> 0 us
  local copies, waits for them, and re-layouts: 117 us -> 14.4 us
  other arithmetic: 32.9 us -> 0 us
  starting transfers between devices: 29.5 us -> 0 us
    pallas_call x0 -> x1, Pallas kernels: none -> 203 us  [body(): pl.pallas_call(kernel, out_shape=jax.ShapeDtypeStruct((32, 512, 128), BF)...]
    all_to_all x4 -> x0, waiting for transfers between devices: 160 us -> none  [the longest x1 67.7 us: body(): lax.all_to_all(ocean_field, 'row', split_axis=2, concat_axis=1, tiled=True)]
    dot_general x17 -> x0, matrix products: 122 us -> none  [the longest x8 96.3 us: update(): jnp.einsum('hc,hk->ck', ffn_out, hidden, preferred_element_type=jnp.float32)]
    convert_element_type x8 -> x0, local copies, waits for them, and re-layouts: 61.9 us -> none  [the longest x2 21 us: body(): second_part.astype(jnp.float32)]
    convert_element_type x3 -> x0, other arithmetic: 31.7 us -> none  [the longest x1 12.9 us: body(): (pair.astype(jnp.float32) + third_part.astype(jnp.float32)).astype(jnp.bf...]
    all_to_all x4 -> x0, starting transfers between devices: 29.5 us -> none  [the longest x1 12.6 us: body(): lax.all_to_all(ocean_field, 'row', split_axis=2, concat_axis=1, tiled=True)]
    reshape x6 -> x1, local copies, waits for them, and re-layouts: 35.6 us -> 9.06 us  [body(): return result.reshape(32, 64, 8, 128).transpose(1, 2, 0, 3)]
    unnamed x23 -> x1, local copies, waits for them, and re-layouts: 16 us -> 1.48 us
  transfers between devices with their start and end apart: 4 -> 0, of which waited for: 4 -> 0; matrix products, arithmetic and copies ran while one was open for 26% -> 0% of each run, Pallas kernels for 0% -> 0%
where the time goes in v1:
time: 218 us
  Pallas kernels  203 us (93%)
  local copies, waits for them, and re-layouts  14.4 us (7%)
    pallas_call x1, Pallas kernels, body(): pl.pallas_call(kernel, out_shape=jax.ShapeDtypeStruct((32, 512, 128), BF)...  203 us
    reshape x1, local copies, waits for them, and re-layouts, body(): return result.reshape(32, 64, 8, 128).transpose(1, 2, 0, 3)  9.06 us

profile of v1, /device:TPU:1, one launch (start us, length us, event | category | flops | bytes accessed | tf_op | source)
XLA Modules:
  0.0 217.8 jit_solution(15468432415362002950)
XLA Ops:
  0.0 0.7 broadcast_in_dim.23
  0.7 0.1 broadcast_in_dim.24
  0.8 1.5 copy.18.ffn_out
  2.3 0.8 broadcast_in_dim.20
  3.1 0.1 broadcast_in_dim.21
  3.2 0.8 broadcast_in_dim.25.bias_out
  4.0 1.3 broadcast_in_dim.22.bias_in
  5.3 203.4 %fno_layer.1 = bf16[32,512,128]{2,1,0:T(8,128)(2,1)} custom-call(bf16[64,8,32,128]{3,2,1,0:T(8,128)(2,1)} %x_hbm.1, bf16[2,32,64,64]{3,2,1,0:T(8,128)(2,1)} %s1_hbm.1, bf16[2,32,64,64]{3,2,1,0:T(8,128)(2,1)} %s2_hbm.1, bf16[2,32,64,64]{3,2,1,0:T(8,128)(2,1)} %s3_hbm.1, bf16[64,256]{1,0:T(8,128)(2,1)} %ffn_in.1, bf16[256,64]{1,0:T(8,128)(2,1)} %copy.18.ffn_out, ...), custom_call_target="tpu_custom_call" | custom-call | tf_op jit(solution)/shard_map/fno_layer/pallas_call | solution.py:378
  208.8 9.1 %copy.21 = bf16[32,64,8,128]{3,0,2,1:T(8,128)(2,1)} copy(bf16[32,64,8,128]{3,2,1,0:T(8,128)(2,1)} %bitcast.4) | data formatting | bytes 8388608 | tf_op jit(solution)/shard_map/reshape | solution.py:392

commit v2 on v1

--- a/solution.py
+++ b/solution.py
@@ -48,7 +48,7 @@
                 swap[a, c, b, c, b, a] = 1.0
     swap = swap.reshape(2 * half * rows, 2 * half * rows)
     place = place.reshape(half * rows, half * rows)
-    return [t.astype(ml_dtypes.bfloat16) for t in (fwd_row, inv_row, fwd_col, inv_col, inv_line, swap, place)]
+    return [t.astype(ml_dtypes.bfloat16) for t in (fwd_row, inv_row, fwd_col, inv_col, inv_line, swap, swap.T, place)]
 
 
 def dot(a, b):
@@ -73,10 +73,11 @@
 
 
 def kernel(
-    x_hbm, s1_hbm, s2_hbm, s3_hbm, ffn_in, ffn_out, bias_in, bias_out,
-    fr_hbm, ir_hbm, fc_hbm, ic_hbm, il_hbm, swap, place,
+    x_hbm, s1_hbm, s2_hbm, s3_hbm, fi_hbm, fo_hbm, bi_hbm, bo_hbm,
+    swap_hbm, back_hbm, place_hbm, fr_hbm, ir_hbm, fc_hbm, ic_hbm, il_hbm,
     out_hbm,
-    x, xs, ra, rb, back1, back2, third, spec, mix_w, fr, ir, fc, ic, il,
+    x, xs, ra, rb, back1, back2, third, spec, mix_w, swap, swap_back, place, fr, ir, fc, ic, il,
+    ffn_in, ffn_out, row_in, row_out, bias_in, bias_out,
     widen_in, widen_out, wide_in, wide_out, hidden,
     load_sem, own_sem, out_sem, fwd_s, fwd_r, ret_s, ret_r, cf_s, cf_r, cr_s, cr_r,
 ):
@@ -85,8 +86,9 @@
         pltpu.make_async_copy(src, dst, load_sem.at[i])
         for i, (src, dst) in enumerate(
             [
-                (x_hbm, x), (s3_hbm, mix_w.at[0]), (fc_hbm, fc), (il_hbm, il), (fr_hbm, fr),
-                (ir_hbm, ir), (ic_hbm, ic), (s1_hbm, mix_w.at[1]), (s2_hbm, mix_w.at[2]),
+                (x_hbm, x), (swap_hbm, swap), (s3_hbm, mix_w.at[0]), (fc_hbm, fc), (il_hbm, il), (place_hbm, place),
+                (fi_hbm, ffn_in), (fo_hbm, ffn_out), (bi_hbm, row_in), (bo_hbm, row_out), (fr_hbm, fr),
+                (ir_hbm, ir), (ic_hbm, ic), (s1_hbm, mix_w.at[1]), (s2_hbm, mix_w.at[2]), (back_hbm, swap_back),
             ]
         )
     ]
@@ -141,6 +143,7 @@
         loop(16, step, 2)
 
     loads[0].wait()
+    loads[1].wait()
     to_rows(0)
     pl.semaphore_wait(barrier, 18)
     for d in ORDER:
@@ -225,7 +228,7 @@
 
         loop(8, behind)
 
-    for i in (1, 2, 3):
+    for i in range(2, 10):
         loads[i].wait()
     branch_third(0)
     branch_third(1)
@@ -241,7 +244,7 @@
         return (b % 8 == a).astype(F32)
 
     widen_in[...] = dot_tn(ffn_in[...], spread(64, 512))
-    widen_out[...] = dot_tn(ffn_out[...], spread(256, 2048))
+    widen_out[...] = dot(ffn_out[...], spread(256, 2048))
 
     def widen(src, dst, columns):
         keep = diagonal(columns)
@@ -255,7 +258,19 @@
     loop(128, widen(widen_in, wide_in, 512))
     loop(32, widen(widen_out, wide_out, 2048))
 
-    for i in range(4, 9):
+    def spread_bias(src, dst, count):
+        def step(i):
+            rows = lax.broadcasted_iota(jnp.int32, (256, count), 0) + 256 * i
+            picked = lax.broadcasted_iota(jnp.int32, (256, count), 1) == rows // 8
+            values = jnp.where(picked, jnp.broadcast_to(src[...], (256, count)), 0.0)
+            dst[pl.ds(256 * i, 256), :] = jnp.broadcast_to(jnp.sum(values, axis=1, keepdims=True), (256, 128))
+
+        loop(8 * count // 256, step)
+
+    spread_bias(row_in, bias_in, 256)
+    spread_bias(row_out, bias_out, 64)
+
+    for i in range(10, 16):
         loads[i].wait()
 
     def do_first(k):
@@ -307,24 +322,33 @@
         summed = jnp.concatenate(lanes, axis=1)
 
         def up(i):
-            at = pl.ds(256 * i, 256)
+            at = pl.ds(512 * i, 512)
             pre = dot(wide_in[at, :], summed)
             bias = bias_in[at, :]
             pre = pre + jnp.concatenate([bias, bias], axis=1)
             hidden[at, :] = (0.5 * pre * (1.0 + lax.erf(pre * ROOT_HALF))).astype(BF)
 
-        loop(8, up)
-
-        def down(i):
-            at = pl.ds(128 * i, 128)
-            result = dot(wide_out[at, :], hidden[...])
-            for j, n in enumerate(both):
-                part = result[:, 128 * j : 128 * (j + 1)] + bias_out[at, :] + xs[n, at, :].astype(F32)
-                xs[n, at, :] = part.astype(BF)
-
-        loop(4, down)
-        for n in both:
-            pltpu.make_async_copy(xs.at[n], out_hbm.at[n], out_sem.at[n]).start()
+        loop(4, up)
+
+        result = dot(wide_out[...], hidden[...])
+        for j, n in enumerate(both):
+            part = result[:, 128 * j : 128 * (j + 1)] + bias_out[...] + xs[n].astype(F32)
+            xs[n] = part.astype(BF)
+
+    def out_copy(k, i):
+        at = (pl.ds(4 * i, 4), slice(None), pl.ds(16 * k, 16), slice(None))
+        return pltpu.make_async_copy(x.at[at], out_hbm.at[at], out_sem.at[k, i])
+
+    def to_cells(k):
+        def step(i):
+            parts = [xs[pl.ds(16 * k, 16), pl.ds(32 * i + 16 * j, 16), :].reshape(256, 128) for j in range(2)]
+            both = dot(swap_back[...], jnp.concatenate(parts, axis=1))
+            for j in range(2):
+                cells = both[:, 128 * j : 128 * (j + 1)].astype(BF).reshape(2, 8, 16, 128)
+                x[pl.ds(4 * i + 2 * j, 2), :, pl.ds(16 * k, 16), :] = cells
+            out_copy(k, i).start()
+
+        loop(16, step, 2)
 
     for k in range(2):
         own_back[k].wait()
@@ -335,9 +359,10 @@
                 if d:
                     give(k, r, s).wait_recv()
             feed(16 * k + sources[0], 16 * k + sources[1])
-
-    for n in range(32):
-        pltpu.make_async_copy(xs.at[n], out_hbm.at[n], out_sem.at[n]).wait()
+        to_cells(k)
+
+    for k in range(2):
+        loop(16, lambda i: out_copy(k, i).wait())
     for k in range(2):
         for d in range(1, 4):
             col_give(k, lax.rem(q + d, 4), q).wait_send()
@@ -347,9 +372,8 @@
 
 def body(ocean_field, spec_first, spec_second, spec_third, ffn_in, ffn_out, bias_in, bias_out):
     consts = constants(128, 32, 8, 16, 16)
-    wide_bias_in = jnp.broadcast_to(jnp.repeat(bias_in, 8)[:, None], (2048, 128))
-    wide_bias_out = jnp.broadcast_to(jnp.repeat(bias_out, 8)[:, None], (512, 128))
-    anywhere, vmem = pl.BlockSpec(memory_space=pl.ANY), pl.BlockSpec(memory_space=pltpu.VMEM)
+    fwd_row, inv_row, fwd_col, inv_col, inv_line, swap, swap_back, place = (jnp.asarray(c) for c in consts)
+    anywhere = pl.BlockSpec(memory_space=pl.ANY)
     dma = pltpu.SemaphoreType.DMA
     scratch = [
         pltpu.VMEM((64, 8, 32, 128), BF),
@@ -361,24 +385,33 @@
         pltpu.VMEM((32, 512, 128), BF),
         pltpu.VMEM((64, 64, 128), F32),
         pltpu.VMEM((3, 2, 32, 64, 64), BF),
+        pltpu.VMEM((256, 256), BF),
+        pltpu.VMEM((256, 256), BF),
+        pltpu.VMEM((128, 128), BF),
         pltpu.VMEM((512, 1024), BF),
         pltpu.VMEM((1024, 512), BF),
         pltpu.VMEM((512, 1024), BF),
         pltpu.VMEM((1024, 512), BF),
         pltpu.VMEM((512, 1024), BF),
+        pltpu.VMEM((64, 256), BF),
+        pltpu.VMEM((64, 256), BF),
+        pltpu.VMEM((1, 256), F32),
+        pltpu.VMEM((1, 64), F32),
+        pltpu.VMEM((2048, 128), F32),
+        pltpu.VMEM((512, 128), F32),
         pltpu.VMEM((256, 512), F32),
         pltpu.VMEM((64, 2048), F32),
         pltpu.VMEM((2048, 512), BF),
         pltpu.VMEM((512, 2048), BF),
         pltpu.VMEM((2048, 256), BF),
-        dma((9,)), dma((8,)), dma((32,)),
+        dma((16,)), dma((8,)), dma((2, 16)),
         dma((2, 16)), dma((2, 16)), dma((2, 16)), dma((2, 16)),
         dma((2, 4)), dma((2, 4)), dma((2, 4)), dma((2, 4)),
     ]
-    result = pl.pallas_call(
+    return pl.pallas_call(
         kernel,
-        out_shape=jax.ShapeDtypeStruct((32, 512, 128), BF),
-        in_specs=[anywhere] * 4 + [vmem] * 4 + [anywhere] * 5 + [vmem] * 2,
+        out_shape=jax.ShapeDtypeStruct(ocean_field.shape, BF),
+        in_specs=[anywhere] * 16,
         out_specs=anywhere,
         scratch_shapes=scratch,
         compiler_params=pltpu.CompilerParams(
@@ -386,10 +419,9 @@
         ),
         name="fno_layer",
     )(
-        ocean_field, spec_first, spec_second, spec_third, ffn_in, ffn_out, wide_bias_in, wide_bias_out,
-        *[jnp.asarray(c) for c in consts],
+        ocean_field, spec_first, spec_second, spec_third, ffn_in, ffn_out.T, bias_in[None, :], bias_out[None, :],
+        swap, swap_back, place, fwd_row, inv_row, fwd_col, inv_col, inv_line,
     )
-    return result.reshape(32, 64, 8, 128).transpose(1, 2, 0, 3)
 
 
 def solution(mesh):

time: 218 us -> 206 us (0.945)
  local copies, waits for them, and re-layouts: 14.4 us -> 5.53 us
  Pallas kernels: 203 us -> 200 us
    reshape x1 -> x0, local copies, waits for them, and re-layouts: 9.06 us -> none  [body(): return result.reshape(32, 64, 8, 128).transpose(1, 2, 0, 3)]
    unnamed x1, local copies, waits for them, and re-layouts: 1.48 us -> 5.53 us
    broadcast_in_dim x6 -> x0, local copies, waits for them, and re-layouts: 3.82 us -> none  [the longest x2 1.41 us: body(): jnp.broadcast_to(jnp.repeat(bias_in, 8)[:, None], (2048, 128))]
    pallas_call x1, Pallas kernels: 203 us -> 200 us  [body(): pl.pallas_call(kernel, out_shape=jax.ShapeDtypeStruct(ocean_field.shape,...]
where the time goes in v2:
time: 206 us
  Pallas kernels  200 us (97%)
  local copies, waits for them, and re-layouts  5.53 us (3%)
    pallas_call x1, Pallas kernels, body(): pl.pallas_call(kernel, out_shape=jax.ShapeDtypeStruct(ocean_field.shape,...  200 us
    unnamed x1, local copies, waits for them, and re-layouts  5.53 us

profile of v2, /device:TPU:1, one launch (start us, length us, event | category | flops | bytes accessed | tf_op | source)
XLA Modules:
  0.0 205.7 jit_solution(14387497710364663324)
XLA Ops:
  0.0 200.2 %fno_layer.1 = bf16[64,8,32,128]{3,2,1,0:T(8,128)(2,1)} custom-call(bf16[64,8,32,128]{3,2,1,0:T(8,128)(2,1)} %x_hbm.1, bf16[2,32,64,64]{3,2,1,0:T(8,128)(2,1)} %s1_hbm.1, bf16[2,32,64,64]{3,2,1,0:T(8,128)(2,1)} %s2_hbm.1, bf16[2,32,64,64]{3,2,1,0:T(8,128)(2,1)} %s3_hbm.1, bf16[64,256]{1,0:T(8,128)(2,1)} %fi_hbm.1, bf16[64,256]{1,0:T(8,128)(2,1)} %bitcast.3, ...), custom_call_target="tpu_custom_call" | custom-call | tf_op jit(solution)/shard_map/fno_layer/pallas_call | solution.py:411
  200.2 5.5 %copy.18 = bf16[64,8,32,128]{3,2,1,0:T(8,128)(2,1)} copy(bf16[64,8,32,128]{3,2,1,0:T(8,128)(2,1)} %fno_layer.1) | data formatting | bytes 8388608

commit v3 on v2

--- a/solution.py
+++ b/solution.py
@@ -72,10 +72,50 @@
     lax.fori_loop(0, count // wide, step, 0)
 
 
+def restored(swap_back, blocks):
+    both = dot(swap_back[...], jnp.concatenate([b.reshape(256, 128) for b in blocks], axis=1))
+    return [both[:, 128 * j : 128 * (j + 1)].astype(BF).reshape(2, 8, 16, 128) for j in range(2)]
+
+
+def finish(back_hbm, cells, rows, out, swap_back, held, staged, table_sem, cell_sem, load_sem, out_sem):
+    table = pltpu.make_async_copy(back_hbm, swap_back, table_sem)
+
+    def load(i):
+        at = (slice(None), pl.ds(64 * i, 64))
+        return pltpu.make_async_copy(rows.at[at], held.at[at], load_sem.at[i])
+
+    def move(i):
+        at = pl.ds(8 * i, 8)
+        return pltpu.make_async_copy(cells.at[at], staged.at[at, :, 0:16], cell_sem.at[i])
+
+    def store(i):
+        at = pl.ds(8 * i, 8)
+        return pltpu.make_async_copy(staged.at[at], out.at[at], out_sem.at[i])
+
+    table.start()
+    for i in range(8):
+        load(i).start()
+        move(i).start()
+    table.wait()
+
+    def step(i):
+        load(i).wait()
+        for e in range(2):
+            blocks = [held[:, pl.ds(64 * i + 32 * e + 16 * j, 16), :] for j in range(2)]
+            for j, part in enumerate(restored(swap_back, blocks)):
+                staged[pl.ds(8 * i + 4 * e + 2 * j, 2), :, 16:32, :] = part
+        move(i).wait()
+        store(i).start()
+
+    loop(8, step, 2)
+    for i in range(8):
+        store(i).wait()
+
+
 def kernel(
     x_hbm, s1_hbm, s2_hbm, s3_hbm, fi_hbm, fo_hbm, bi_hbm, bo_hbm,
     swap_hbm, back_hbm, place_hbm, fr_hbm, ir_hbm, fc_hbm, ic_hbm, il_hbm,
-    out_hbm,
+    out_cells, out_rows,
     x, xs, ra, rb, back1, back2, third, spec, mix_w, swap, swap_back, place, fr, ir, fc, ic, il,
     ffn_in, ffn_out, row_in, row_out, bias_in, bias_out,
     widen_in, widen_out, wide_in, wide_out, hidden,
@@ -86,7 +126,7 @@
         pltpu.make_async_copy(src, dst, load_sem.at[i])
         for i, (src, dst) in enumerate(
             [
-                (x_hbm, x), (swap_hbm, swap), (s3_hbm, mix_w.at[0]), (fc_hbm, fc), (il_hbm, il), (place_hbm, place),
+                (x_hbm.at[:32], x.at[:32]), (swap_hbm, swap), (x_hbm.at[32:], x.at[32:]), (s3_hbm, mix_w.at[0]), (fc_hbm, fc), (il_hbm, il), (place_hbm, place),
                 (fi_hbm, ffn_in), (fo_hbm, ffn_out), (bi_hbm, row_in), (bo_hbm, row_out), (fr_hbm, fr),
                 (ir_hbm, ir), (ic_hbm, ic), (s1_hbm, mix_w.at[1]), (s2_hbm, mix_w.at[2]), (back_hbm, swap_back),
             ]
@@ -101,10 +141,14 @@
     for d in range(1, 4):
         pl.semaphore_signal(barrier, inc=1, device_id=(g, r, lax.rem(q + d, 4)), device_id_type=MESH)
 
-    def forward(k, t, s):
+    def forward(part, t, s):
+        k, at = ((0, pl.ds(0, 256)), (0, pl.ds(256, 256)), (1, pl.ds(0, 512)))[part]
         return pltpu.make_async_remote_copy(
-            xs.at[k * 16 + t], ra.at[k, s], fwd_s.at[k, t], fwd_r.at[k, s], device_id=(g, t, q), device_id_type=MESH
+            xs.at[k * 16 + t, at], ra.at[k, s, at], fwd_s.at[part, t], fwd_r.at[part, s],
+            device_id=(g, t, q), device_id_type=MESH,
         )
+
+    parts_of = ((0, 1), (2,))
 
     def give(k, t, s):
         return pltpu.make_async_remote_copy(
@@ -135,27 +179,31 @@
         both = dot(swap[...], jnp.concatenate(parts, axis=1))
         return [both[:, 128 * j : 128 * (j + 1)].reshape(16, 16, 128) for j in range(2)]
 
-    def to_rows(k):
+    def to_rows(k, start, count):
         def step(i):
-            for j, part in enumerate(swapped(x, k, i)):
-                xs[pl.ds(16 * k, 16), pl.ds(32 * i + 16 * j, 16), :] = part.astype(BF)
-
-        loop(16, step, 2)
+            for j, part in enumerate(swapped(x, k, start + i)):
+                xs[pl.ds(16 * k, 16), pl.ds(32 * (start + i) + 16 * j, 16), :] = part.astype(BF)
+
+        loop(count, step, 4)
 
     loads[0].wait()
     loads[1].wait()
-    to_rows(0)
+    to_rows(0, 0, 8)
     pl.semaphore_wait(barrier, 18)
     for d in ORDER:
         forward(0, lax.rem(r + d, 16), r).start()
+    loads[2].wait()
+    to_rows(0, 8, 8)
+    for d in ORDER:
+        forward(1, lax.rem(r + d, 16), r).start()
     own[0].start()
     for k in range(2):
         own_col[k].start()
         for d in range(1, 4):
             col_forward(k, lax.rem(q + d, 4), q).start()
-    to_rows(1)
+    to_rows(1, 0, 16)
     for d in ORDER:
-        forward(1, lax.rem(r + d, 16), r).start()
+        forward(2, lax.rem(r + d, 16), r).start()
     own[1].start()
 
     def transposed_mix(d):
@@ -228,7 +276,7 @@
 
         loop(8, behind)
 
-    for i in range(2, 10):
+    for i in range(3, 11):
         loads[i].wait()
     branch_third(0)
     branch_third(1)
@@ -270,13 +318,14 @@
     spread_bias(row_in, bias_in, 256)
     spread_bias(row_out, bias_out, 64)
 
-    for i in range(10, 16):
+    for i in range(11, 17):
         loads[i].wait()
 
     def do_first(k):
         own[k].wait()
-        for d in ORDER:
-            forward(k, r, lax.rem(r + 16 - d, 16)).wait_recv()
+        for part in parts_of[k]:
+            for d in ORDER:
+                forward(part, r, lax.rem(r + 16 - d, 16)).wait_recv()
         branch_first(k)
         for d in ORDER:
             give(k, lax.rem(r + d, 16), r).start()
@@ -302,8 +351,9 @@
             col_give(k, q, lax.rem(q + d, 4)).wait_recv()
         for d in range(1, 4):
             col_forward(k, lax.rem(q + d, 4), q).wait_send()
-        for d in ORDER:
-            forward(k, lax.rem(r + d, 16), r).wait_send()
+        for part in parts_of[k]:
+            for d in ORDER:
+                forward(part, lax.rem(r + d, 16), r).wait_send()
 
     def add_second(k):
         def step(i):
@@ -311,7 +361,7 @@
                 at = (pl.ds(16 * k, 16), pl.ds(32 * i + 16 * j, 16), slice(None))
                 third[at] = (third[at].astype(F32) + part).astype(BF)
 
-        loop(16, step, 2)
+        loop(16, step, 4)
 
     add_second(0)
     add_second(1)
@@ -328,41 +378,47 @@
             pre = pre + jnp.concatenate([bias, bias], axis=1)
             hidden[at, :] = (0.5 * pre * (1.0 + lax.erf(pre * ROOT_HALF))).astype(BF)
 
-        loop(4, up)
+        loop(4, up, 2)
 
         result = dot(wide_out[...], hidden[...])
         for j, n in enumerate(both):
             part = result[:, 128 * j : 128 * (j + 1)] + bias_out[...] + xs[n].astype(F32)
             xs[n] = part.astype(BF)
 
-    def out_copy(k, i):
-        at = (pl.ds(4 * i, 4), slice(None), pl.ds(16 * k, 16), slice(None))
-        return pltpu.make_async_copy(x.at[at], out_hbm.at[at], out_sem.at[k, i])
-
-    def to_cells(k):
-        def step(i):
-            parts = [xs[pl.ds(16 * k, 16), pl.ds(32 * i + 16 * j, 16), :].reshape(256, 128) for j in range(2)]
-            both = dot(swap_back[...], jnp.concatenate(parts, axis=1))
-            for j in range(2):
-                cells = both[:, 128 * j : 128 * (j + 1)].astype(BF).reshape(2, 8, 16, 128)
-                x[pl.ds(4 * i + 2 * j, 2), :, pl.ds(16 * k, 16), :] = cells
-            out_copy(k, i).start()
-
-        loop(16, step, 2)
+    def out_copy(i):
+        at = (pl.ds(4 * i, 4), slice(None), pl.ds(0, 16), slice(None))
+        return pltpu.make_async_copy(x.at[at], out_cells.at[pl.ds(4 * i, 4)], out_sem.at[i])
+
+    def row_copy(n):
+        return pltpu.make_async_copy(xs.at[16 + n], out_rows.at[n], out_sem.at[16 + n])
+
+    def to_cells(i):
+        for j, cells in enumerate(restored(swap_back, [xs[pl.ds(0, 16), pl.ds(32 * i + 16 * j, 16), :] for j in range(2)])):
+            x[pl.ds(4 * i + 2 * j, 2), :, pl.ds(0, 16), :] = cells
+        out_copy(i).start()
 
     for k in range(2):
         own_back[k].wait()
-        steps = (0,) + ORDER
-        for i in range(8):
-            sources = [lax.rem(r + 16 - d, 16) for d in steps[2 * i : 2 * i + 2]]
-            for d, s in zip(steps[2 * i : 2 * i + 2], sources):
-                if d:
-                    give(k, r, s).wait_recv()
+
+        def unit(i):
+            sources = [lax.rem(r + 16 - lax.rem(8 - i, 8), 16), lax.rem(r + 8 - i, 16)]
+
+            @pl.when(i > 0)
+            def _():
+                give(k, r, sources[0]).wait_recv()
+
+            give(k, r, sources[1]).wait_recv()
             feed(16 * k + sources[0], 16 * k + sources[1])
-        to_cells(k)
-
-    for k in range(2):
-        loop(16, lambda i: out_copy(k, i).wait())
+            if k == 1:
+                row_copy(sources[0]).start()
+                row_copy(sources[1]).start()
+
+        loop(8, unit)
+        if k == 0:
+            loop(16, to_cells, 4)
+
+    loop(16, lambda i: out_copy(i).wait())
+    loop(16, lambda i: row_copy(i).wait())
     for k in range(2):
         for d in range(1, 4):
             col_give(k, lax.rem(q + d, 4), q).wait_send()
@@ -404,15 +460,15 @@
         pltpu.VMEM((2048, 512), BF),
         pltpu.VMEM((512, 2048), BF),
         pltpu.VMEM((2048, 256), BF),
-        dma((16,)), dma((8,)), dma((2, 16)),
-        dma((2, 16)), dma((2, 16)), dma((2, 16)), dma((2, 16)),
+        dma((17,)), dma((8,)), dma((32,)),
+        dma((3, 16)), dma((3, 16)), dma((2, 16)), dma((2, 16)),
         dma((2, 4)), dma((2, 4)), dma((2, 4)), dma((2, 4)),
     ]
-    return pl.pallas_call(
+    cells, rows = pl.pallas_call(
         kernel,
-        out_shape=jax.ShapeDtypeStruct(ocean_field.shape, BF),
+        out_shape=(jax.ShapeDtypeStruct((64, 8, 16, 128), BF), jax.ShapeDtypeStruct((16, 512, 128), BF)),
         in_specs=[anywhere] * 16,
-        out_specs=anywhere,
+        out_specs=(anywhere, anywhere),
         scratch_shapes=scratch,
         compiler_params=pltpu.CompilerParams(
             collective_id=0, has_side_effects=True, vmem_limit_bytes=60 * 2**20
@@ -422,6 +478,19 @@
         ocean_field, spec_first, spec_second, spec_third, ffn_in, ffn_out.T, bias_in[None, :], bias_out[None, :],
         swap, swap_back, place, fwd_row, inv_row, fwd_col, inv_col, inv_line,
     )
+    return pl.pallas_call(
+        finish,
+        out_shape=jax.ShapeDtypeStruct(ocean_field.shape, BF),
+        in_specs=[anywhere] * 3,
+        out_specs=anywhere,
+        scratch_shapes=[
+            pltpu.VMEM((256, 256), BF),
+            pltpu.VMEM((16, 512, 128), BF),
+            pltpu.VMEM((64, 8, 32, 128), BF),
+            dma(()), dma((8,)), dma((8,)), dma((8,)),
+        ],
+        name="finish",
+    )(swap_back, cells, rows)
 
 
 def solution(mesh):

time: 206 us -> 202 us (0.981)
  local copies, waits for them, and re-layouts: 5.53 us -> 0 us
    unnamed x1 -> x0, local copies, waits for them, and re-layouts: 5.53 us -> none
    pallas_call x1 -> x2, Pallas kernels: 200 us -> 202 us  [the longest x1 197 us: body(): pl.pallas_call(kernel, out_shape=(jax.ShapeDtypeStruct((64, 8, 16, 128),...]
where the time goes in v3:
time: 202 us
  Pallas kernels  202 us (100%)
    pallas_call x1, Pallas kernels, body(): pl.pallas_call(kernel, out_shape=(jax.ShapeDtypeStruct((64, 8, 16, 128),...  197 us
    pallas_call x1, Pallas kernels, body(): pl.pallas_call(finish, out_shape=jax.ShapeDtypeStruct(ocean_field.shape,...  4.94 us

profile of v3, /device:TPU:1, one launch (start us, length us, event | category | flops | bytes accessed | tf_op | source)
XLA Modules:
  0.0 201.9 jit_solution(5084273637050503324)
XLA Ops:
  0.0 197.0 %fno_layer.1 = (bf16[64,8,16,128]{3,2,1,0:T(8,128)(2,1)}, bf16[16,512,128]{2,1,0:T(8,128)(2,1)}) custom-call(bf16[64,8,32,128]{3,2,1,0:T(8,128)(2,1)} %x_hbm.1, bf16[2,32,64,64]{3,2,1,0:T(8,128)(2,1)} %s1_hbm.1, bf16[2,32,64,64]{3,2,1,0:T(8,128)(2,1)} %s2_hbm.1, bf16[2,32,64,64]{3,2,1,0:T(8,128)(2,1)} %s3_hbm.1, bf16[64,256]{1,0:T(8,128)(2,1)} %fi_hbm.1, ...), custom_call_target="tpu_custom_call" | custom-call | tf_op jit(solution)/shard_map/fno_layer/pallas_call | solution.py:467
  197.0 4.9 %finish.1 = bf16[64,8,32,128]{3,2,1,0:T(8,128)(2,1)} custom-call(bf16[256,256]{1,0:T(8,128)(2,1)} %constant.19.clone.swap_hbm.back_hbm, bf16[64,8,16,128]{3,2,1,0:T(8,128)(2,1)} %get-tuple-element.7.cells, bf16[16,512,128]{2,1,0:T(8,128)(2,1)} %get-tuple-element.8.rows), custom_call_target="tpu_custom_call" | custom-call | tf_op jit(solution)/shard_map/finish/pallas_call | solution.py:481

commit v4 on v3

--- a/solution.py
+++ b/solution.py
@@ -81,34 +81,34 @@
     table = pltpu.make_async_copy(back_hbm, swap_back, table_sem)
 
     def load(i):
-        at = (slice(None), pl.ds(64 * i, 64))
+        at = (slice(None), pl.ds(128 * i, 128))
         return pltpu.make_async_copy(rows.at[at], held.at[at], load_sem.at[i])
 
     def move(i):
-        at = pl.ds(8 * i, 8)
+        at = pl.ds(16 * i, 16)
         return pltpu.make_async_copy(cells.at[at], staged.at[at, :, 0:16], cell_sem.at[i])
 
     def store(i):
-        at = pl.ds(8 * i, 8)
+        at = pl.ds(16 * i, 16)
         return pltpu.make_async_copy(staged.at[at], out.at[at], out_sem.at[i])
 
     table.start()
-    for i in range(8):
+    for i in range(4):
         load(i).start()
         move(i).start()
     table.wait()
 
     def step(i):
         load(i).wait()
-        for e in range(2):
-            blocks = [held[:, pl.ds(64 * i + 32 * e + 16 * j, 16), :] for j in range(2)]
+        for e in range(4):
+            blocks = [held[:, pl.ds(128 * i + 32 * e + 16 * j, 16), :] for j in range(2)]
             for j, part in enumerate(restored(swap_back, blocks)):
-                staged[pl.ds(8 * i + 4 * e + 2 * j, 2), :, 16:32, :] = part
+                staged[pl.ds(16 * i + 4 * e + 2 * j, 2), :, 16:32, :] = part
         move(i).wait()
         store(i).start()
 
-    loop(8, step, 2)
-    for i in range(8):
+    loop(4, step)
+    for i in range(4):
         store(i).wait()
 
 
@@ -327,7 +327,7 @@
             for d in ORDER:
                 forward(part, r, lax.rem(r + 16 - d, 16)).wait_recv()
         branch_first(k)
-        for d in ORDER:
+        for d in ORDER[::-1]:
             give(k, lax.rem(r + d, 16), r).start()
         own_back[k].start()
 
@@ -401,9 +401,9 @@
         own_back[k].wait()
 
         def unit(i):
-            sources = [lax.rem(r + 16 - lax.rem(8 - i, 8), 16), lax.rem(r + 8 - i, 16)]
-
-            @pl.when(i > 0)
+            sources = [lax.rem(r + 16 - lax.rem(i + 1, 8), 16), lax.rem(r + 1 + i, 16)]
+
+            @pl.when(i < 7)
             def _():
                 give(k, r, sources[0]).wait_recv()
 
@@ -487,7 +487,7 @@
             pltpu.VMEM((256, 256), BF),
             pltpu.VMEM((16, 512, 128), BF),
             pltpu.VMEM((64, 8, 32, 128), BF),
-            dma(()), dma((8,)), dma((8,)), dma((8,)),
+            dma(()), dma((4,)), dma((4,)), dma((4,)),
         ],
         name="finish",
     )(swap_back, cells, rows)

time: 202 us -> 199 us (0.985)
  Pallas kernels: 202 us -> 198 us
    pallas_call x1, Pallas kernels: 197 us -> 193 us  [body(): pl.pallas_call(kernel, out_shape=(jax.ShapeDtypeStruct((64, 8, 16, 128),...]
where the time goes in v4:
time: 199 us; the launch traced here: 198 us
  Pallas kernels  198 us (99%)
    pallas_call x1, Pallas kernels, body(): pl.pallas_call(kernel, out_shape=(jax.ShapeDtypeStruct((64, 8, 16, 128),...  193 us
    pallas_call x1, Pallas kernels, body(): pl.pallas_call(finish, out_shape=jax.ShapeDtypeStruct(ocean_field.shape,...  4.28 us

profile of v4, /device:TPU:1, one launch (start us, length us, event | category | flops | bytes accessed | tf_op | source)
XLA Modules:
  0.0 197.7 jit_solution(979516362598776425)
XLA Ops:
  0.0 193.4 %fno_layer.1 = (bf16[64,8,16,128]{3,2,1,0:T(8,128)(2,1)}, bf16[16,512,128]{2,1,0:T(8,128)(2,1)}) custom-call(bf16[64,8,32,128]{3,2,1,0:T(8,128)(2,1)} %x_hbm.1, bf16[2,32,64,64]{3,2,1,0:T(8,128)(2,1)} %s1_hbm.1, bf16[2,32,64,64]{3,2,1,0:T(8,128)(2,1)} %s2_hbm.1, bf16[2,32,64,64]{3,2,1,0:T(8,128)(2,1)} %s3_hbm.1, bf16[64,256]{1,0:T(8,128)(2,1)} %fi_hbm.1, ...), custom_call_target="tpu_custom_call" | custom-call | tf_op jit(solution)/shard_map/fno_layer/pallas_call | solution.py:467
  193.4 4.3 %finish.1 = bf16[64,8,32,128]{3,2,1,0:T(8,128)(2,1)} custom-call(bf16[256,256]{1,0:T(8,128)(2,1)} %constant.19.clone.swap_hbm.back_hbm, bf16[64,8,16,128]{3,2,1,0:T(8,128)(2,1)} %get-tuple-element.7.cells, bf16[16,512,128]{2,1,0:T(8,128)(2,1)} %get-tuple-element.8.rows), custom_call_target="tpu_custom_call" | custom-call | tf_op jit(solution)/shard_map/finish/pallas_call | solution.py:481

commit v5 on v4

--- a/solution.py
+++ b/solution.py
@@ -126,7 +126,7 @@
         pltpu.make_async_copy(src, dst, load_sem.at[i])
         for i, (src, dst) in enumerate(
             [
-                (x_hbm.at[:32], x.at[:32]), (swap_hbm, swap), (x_hbm.at[32:], x.at[32:]), (s3_hbm, mix_w.at[0]), (fc_hbm, fc), (il_hbm, il), (place_hbm, place),
+                (x_hbm.at[:16], x.at[:16]), (swap_hbm, swap), (x_hbm.at[16:], x.at[16:]), (s3_hbm, mix_w.at[0]), (fc_hbm, fc), (il_hbm, il), (place_hbm, place),
                 (fi_hbm, ffn_in), (fo_hbm, ffn_out), (bi_hbm, row_in), (bo_hbm, row_out), (fr_hbm, fr),
                 (ir_hbm, ir), (ic_hbm, ic), (s1_hbm, mix_w.at[1]), (s2_hbm, mix_w.at[2]), (back_hbm, swap_back),
             ]
@@ -142,7 +142,7 @@
         pl.semaphore_signal(barrier, inc=1, device_id=(g, r, lax.rem(q + d, 4)), device_id_type=MESH)
 
     def forward(part, t, s):
-        k, at = ((0, pl.ds(0, 256)), (0, pl.ds(256, 256)), (1, pl.ds(0, 512)))[part]
+        k, at = ((0, pl.ds(0, 128)), (0, pl.ds(128, 384)), (1, pl.ds(0, 512)))[part]
         return pltpu.make_async_remote_copy(
             xs.at[k * 16 + t, at], ra.at[k, s, at], fwd_s.at[part, t], fwd_r.at[part, s],
             device_id=(g, t, q), device_id_type=MESH,
@@ -188,12 +188,12 @@
 
     loads[0].wait()
     loads[1].wait()
-    to_rows(0, 0, 8)
+    to_rows(0, 0, 4)
     pl.semaphore_wait(barrier, 18)
     for d in ORDER:
         forward(0, lax.rem(r + d, 16), r).start()
     loads[2].wait()
-    to_rows(0, 8, 8)
+    to_rows(0, 4, 12)
     for d in ORDER:
         forward(1, lax.rem(r + d, 16), r).start()
     own[0].start()

time: 199 us -> 199 us (level)
  no operation moved by 1% of the time
where the time goes in v5:
time: 199 us; the launch traced here: 198 us
  Pallas kernels  198 us (99%)
    pallas_call x1, Pallas kernels, body(): pl.pallas_call(kernel, out_shape=(jax.ShapeDtypeStruct((64, 8, 16, 128),...  193 us
    pallas_call x1, Pallas kernels, body(): pl.pallas_call(finish, out_shape=jax.ShapeDtypeStruct(ocean_field.shape,...  4.28 us

profile of v5, /device:TPU:1, one launch (start us, length us, event | category | flops | bytes accessed | tf_op | source)
XLA Modules:
  0.0 197.6 jit_solution(1891801743017934070)
XLA Ops:
  0.0 193.3 %fno_layer.1 = (bf16[64,8,16,128]{3,2,1,0:T(8,128)(2,1)}, bf16[16,512,128]{2,1,0:T(8,128)(2,1)}) custom-call(bf16[64,8,32,128]{3,2,1,0:T(8,128)(2,1)} %x_hbm.1, bf16[2,32,64,64]{3,2,1,0:T(8,128)(2,1)} %s1_hbm.1, bf16[2,32,64,64]{3,2,1,0:T(8,128)(2,1)} %s2_hbm.1, bf16[2,32,64,64]{3,2,1,0:T(8,128)(2,1)} %s3_hbm.1, bf16[64,256]{1,0:T(8,128)(2,1)} %fi_hbm.1, ...), custom_call_target="tpu_custom_call" | custom-call | tf_op jit(solution)/shard_map/fno_layer/pallas_call | solution.py:467
  193.3 4.3 %finish.1 = bf16[64,8,32,128]{3,2,1,0:T(8,128)(2,1)} custom-call(bf16[256,256]{1,0:T(8,128)(2,1)} %constant.19.clone.swap_hbm.back_hbm, bf16[64,8,16,128]{3,2,1,0:T(8,128)(2,1)} %get-tuple-element.7.cells, bf16[16,512,128]{2,1,0:T(8,128)(2,1)} %get-tuple-element.8.rows), custom_call_target="tpu_custom_call" | custom-call | tf_op jit(solution)/shard_map/finish/pallas_call | solution.py:481
